TPU v7x, 32 devices: a whole 2x2x4 slice. The times are simulated.
32 devices in a mesh: uly: 4 (over y, x), blk: 8 (over z, core).
Axes of the slice: x: 2, y: 2, z: 4, core: 2. Of those that a mesh axis runs over, the one named last changes fastest.
Arguments:
- video_q: bfloat16 [9216, 3072], P(('blk', 'uly')), may hold values from -16 to 16
- video_k: bfloat16 [9216, 3072], P(('blk', 'uly')), may hold values from -16 to 16
- video_v: bfloat16 [9216, 3072], P(('blk', 'uly')), may hold values from -6 to 6
- text_q: bfloat16 [256, 3072], P('uly'), may hold values from -16 to 16
- text_k: bfloat16 [256, 3072], P('uly'), may hold values from -16 to 16
- text_v: bfloat16 [256, 3072], P('uly'), may hold values from -6 to 6
- window_tiles: int32 [24, 6], P('blk'), may hold values from 0 to 23, as said below
- text_len: int32 [1], replicated, may hold values from 64 to 256
Outputs:
- video_out: bfloat16 [9216, 3072], P(('blk', 'uly'))
- text_out: bfloat16 [256, 3072], P('uly')
Inputs may be any that keep to these rules, and one draw needn't show every extreme that they name: `window_tiles`: tile j lies in time slice j // 3 of 8; row j lists, each once and in any order, the 6 tiles of two consecutive time slices, one of which is the slice of tile j.
All inputs are finite; a program needn't handle non-finite values.
Results may differ from a plain program's by a relative error of at most 0.0036.
Values may be sent and summed in bfloat16 or wider, within the bound.
A program may use at most 128 MiB of HBM per device.

v0:
```python
import math

import jax
import jax.numpy as jnp
from jax import lax
from jax.sharding import PartitionSpec as P

HEADS = 24
D_HEAD = 128
TILE = 384


def passed_along(block, axis, distance):
    devices = range(lax.axis_size(axis))
    route = [(i - distance, i) for i in devices if i - distance in devices]
    return lax.ppermute(block, axis, route)


def split_heads(matrix):
    return matrix.reshape(matrix.shape[0], HEADS, D_HEAD)


def head_major(tensor):
    return jnp.transpose(tensor, (1, 0, 2))


def local(video_q, video_k, video_v, text_q, text_k, text_v, window_tiles, text_len):
    inv_root = 1.0 / math.sqrt(D_HEAD)
    regrouped = (
        lax.all_to_all(split_heads(video_q), "uly", split_axis=1, concat_axis=0, tiled=True),
        lax.all_to_all(split_heads(video_k), "uly", split_axis=1, concat_axis=0, tiled=True),
        lax.all_to_all(split_heads(video_v), "uly", split_axis=1, concat_axis=0, tiled=True),
        lax.all_to_all(split_heads(text_q), "uly", split_axis=1, concat_axis=0, tiled=True),
        lax.all_to_all(split_heads(text_k), "uly", split_axis=1, concat_axis=0, tiled=True),
        lax.all_to_all(split_heads(text_v), "uly", split_axis=1, concat_axis=0, tiled=True),
    )
    own_q, own_k, own_v, text_qh, text_kh, text_vh = regrouped
    head_queries = head_major(own_q)
    own_kv = jnp.stack([head_major(own_k), head_major(own_v)])
    text_queries = head_major(text_qh)
    text_keys = head_major(text_kh)
    text_values = head_major(text_vh)
    beside = []
    for offset in (1, -1):
        beside.append(passed_along(own_kv, "blk", offset))
    blocks = [beside[0], own_kv, beside[1]]
    heads_dev = own_kv.shape[1]
    row_count = own_kv.shape[2]
    tiles_dev = row_count // TILE
    window_size = window_tiles.shape[1]
    gathered = jnp.concatenate(blocks, axis=2).reshape(2, heads_dev, 3 * tiles_dev, TILE, D_HEAD)
    local_tiles = window_tiles - (lax.axis_index("blk") - 1) * tiles_dev
    live_text = jnp.arange(text_keys.shape[1], dtype=jnp.int32) < text_len[0]

    def video_attention(inputs):
        queries, keys_all, values_all, keys_text, values_text = inputs
        keys_win = jnp.take(keys_all, local_tiles, axis=0).reshape(
            tiles_dev, window_size * TILE, D_HEAD
        )
        values_win = jnp.take(values_all, local_tiles, axis=0).reshape(
            tiles_dev, window_size * TILE, D_HEAD
        )
        tile_queries = queries.reshape(tiles_dev, TILE, D_HEAD)
        win_scores = (
            jnp.einsum("tqd,tkd->tqk", tile_queries, keys_win, preferred_element_type=jnp.float32)
            * inv_root
        )
        txt_scores = (
            jnp.einsum("tqd,kd->tqk", tile_queries, keys_text, preferred_element_type=jnp.float32)
            * inv_root
        )
        txt_scores = jnp.where(live_text, txt_scores, -jnp.inf)
        row_top = jnp.maximum(jnp.max(win_scores, axis=2), jnp.max(txt_scores, axis=2))[:, :, None]
        win_weights = jnp.exp(win_scores - row_top)
        txt_weights = jnp.exp(txt_scores - row_top)
        weight_sum = jnp.sum(win_weights, axis=2) + jnp.sum(txt_weights, axis=2)
        numerator = jnp.einsum(
            "tqk,tkd->tqd",
            win_weights.astype(jnp.bfloat16),
            values_win,
            preferred_element_type=jnp.float32,
        )
        numerator = numerator + jnp.einsum(
            "tqk,kd->tqd",
            txt_weights.astype(jnp.bfloat16),
            values_text,
            preferred_element_type=jnp.float32,
        )
        return (numerator / weight_sum[:, :, None]).astype(jnp.bfloat16).reshape(row_count, D_HEAD)

    video_heads = lax.map(
        video_attention, (head_queries, gathered[0], gathered[1], text_keys, text_values)
    )
    vid_scores = (
        jnp.einsum("hqd,hkd->hqk", text_queries, own_kv[0], preferred_element_type=jnp.float32)
        * inv_root
    )
    txt_scores = (
        jnp.einsum("hqd,hkd->hqk", text_queries, text_keys, preferred_element_type=jnp.float32)
        * inv_root
    )
    txt_scores = jnp.where(live_text, txt_scores, -jnp.inf)
    video_top = lax.pmax(jnp.max(vid_scores, axis=2), "blk")
    row_top = jnp.maximum(video_top, jnp.max(txt_scores, axis=2))[:, :, None]
    vid_weights = jnp.exp(vid_scores - row_top)
    vid_numer = jnp.einsum(
        "hqk,hkd->hqd",
        vid_weights.astype(jnp.bfloat16),
        own_kv[1],
        preferred_element_type=jnp.float32,
    )
    vid_total, vid_numer = lax.psum((jnp.sum(vid_weights, axis=2), vid_numer), "blk")
    txt_weights = jnp.exp(txt_scores - row_top)
    weight_sum = vid_total + jnp.sum(txt_weights, axis=2)
    numerator = vid_numer + jnp.einsum(
        "hqk,hkd->hqd",
        txt_weights.astype(jnp.bfloat16),
        text_values,
        preferred_element_type=jnp.float32,
    )
    text_heads = (numerator / weight_sum[:, :, None]).astype(jnp.bfloat16)
    returned = (
        lax.all_to_all(head_major(video_heads), "uly", split_axis=0, concat_axis=1, tiled=True),
        lax.all_to_all(head_major(text_heads), "uly", split_axis=0, concat_axis=1, tiled=True),
    )
    video_out = returned[0].reshape(returned[0].shape[0], HEADS * D_HEAD)
    text_out = returned[1].reshape(returned[1].shape[0], HEADS * D_HEAD)
    return (video_out, text_out)


def solution(mesh):
    in_specs = (
        P(("blk", "uly"), None),
        P(("blk", "uly"), None),
        P(("blk", "uly"), None),
        P("uly", None),
        P("uly", None),
        P("uly", None),
        P("blk", None),
        P(),
    )
    out_specs = (P(("blk", "uly"), None), P("uly", None))
    return jax.shard_map(local, mesh=mesh, in_specs=in_specs, out_specs=out_specs, check_vma=False)
```

profile of v0, /device:TPU:0, one launch (start us, length us, event | category | flops | bytes accessed | tf_op | source)
XLA Modules:
  0.0 382.1 jit_solution(15346188951037126867)
XLA Ops:
  10.2 5.3 %all-to-all-start.1 = ((bf16[288,24,128]{2,0,1:T(8,128)(2,1)}), bf16[288,24,128]{2,0,1:T(8,128)(2,1)S(1)}, u32[]{:S(2)}, u32[]{:S(2)}) async-start(bf16[288,24,128]{2,0,1:T(8,128)(2,1)} %copy_bitcast_fusion.3), calls=%async_computation.1 | async-start | bytes 3538944 | tf_op jit(solution)/shard_map/all_to_all | solution.py:31
  17.0 19.8 %all-to-all-done.1 = bf16[288,24,128]{2,0,1:T(8,128)(2,1)S(1)} async-done(((bf16[288,24,128]{2,0,1:T(8,128)(2,1)}), bf16[288,24,128]{2,0,1:T(8,128)(2,1)S(1)}, u32[]{:S(2)}, u32[]{:S(2)}) %all-to-all-start.1) | async-done | bytes 1769504 | tf_op jit(solution)/shard_map/all_to_all | solution.py:31
  36.8 4.4 %all-to-all-start.2 = ((bf16[288,24,128]{2,0,1:T(8,128)(2,1)}), bf16[288,24,128]{2,0,1:T(8,128)(2,1)}, u32[]{:S(2)}, u32[]{:S(2)}) async-start(bf16[288,24,128]{2,0,1:T(8,128)(2,1)} %copy_bitcast_fusion.2), calls=%async_computation.2 | async-start | bytes 3538944 | tf_op jit(solution)/shard_map/all_to_all | solution.py:32
  41.4 20.7 %all-to-all-done.2 = bf16[288,24,128]{2,0,1:T(8,128)(2,1)} async-done(((bf16[288,24,128]{2,0,1:T(8,128)(2,1)}), bf16[288,24,128]{2,0,1:T(8,128)(2,1)}, u32[]{:S(2)}, u32[]{:S(2)}) %all-to-all-start.2) | async-done | bytes 1769504 | tf_op jit(solution)/shard_map/all_to_all | solution.py:32
  71.2 4.1 %all-to-all-start.6 = ((bf16[64,24,128]{2,0,1:T(8,128)(2,1)}), bf16[64,24,128]{2,0,1:T(8,128)(2,1)}, u32[]{:S(2)}, u32[]{:S(2)}) async-start(bf16[64,24,128]{2,0,1:T(8,128)(2,1)} %copy_bitcast_fusion.6), calls=%async_computation.6 | async-start | bytes 786432 | tf_op jit(solution)/shard_map/all_to_all | solution.py:33
  77.8 5.2 %all-to-all-done.6 = bf16[64,24,128]{2,0,1:T(8,128)(2,1)} async-done(((bf16[64,24,128]{2,0,1:T(8,128)(2,1)}), bf16[64,24,128]{2,0,1:T(8,128)(2,1)}, u32[]{:S(2)}, u32[]{:S(2)}) %all-to-all-start.6) | async-done | bytes 393248 | tf_op jit(solution)/shard_map/all_to_all | solution.py:33
  83.0 4.1 %all-to-all-start.3 = ((bf16[64,24,128]{2,0,1:T(8,128)(2,1)}), bf16[64,24,128]{2,0,1:T(8,128)(2,1)}, u32[]{:S(2)}, u32[]{:S(2)}) async-start(bf16[64,24,128]{2,0,1:T(8,128)(2,1)} %copy_bitcast_fusion.8), calls=%async_computation.3 | async-start | bytes 786432 | tf_op jit(solution)/shard_map/all_to_all | solution.py:34
  89.0 5.4 %all-to-all-done.3 = bf16[64,24,128]{2,0,1:T(8,128)(2,1)} async-done(((bf16[64,24,128]{2,0,1:T(8,128)(2,1)}), bf16[64,24,128]{2,0,1:T(8,128)(2,1)}, u32[]{:S(2)}, u32[]{:S(2)}) %all-to-all-start.3) | async-done | bytes 393248 | tf_op jit(solution)/shard_map/all_to_all | solution.py:34
  94.4 4.1 %all-to-all-start.4 = ((bf16[64,24,128]{2,0,1:T(8,128)(2,1)}), bf16[64,24,128]{2,0,1:T(8,128)(2,1)}, u32[]{:S(2)}, u32[]{:S(2)}) async-start(bf16[64,24,128]{2,0,1:T(8,128)(2,1)} %copy_bitcast_fusion.7), calls=%async_computation.4 | async-start | bytes 786432 | tf_op jit(solution)/shard_map/all_to_all | solution.py:35
  105.1 4.4 %all-to-all-start = ((bf16[288,24,128]{2,0,1:T(8,128)(2,1)}), bf16[288,24,128]{2,0,1:T(8,128)(2,1)}, u32[]{:S(2)}, u32[]{:S(2)}) async-start(bf16[288,24,128]{2,0,1:T(8,128)(2,1)} %copy_bitcast_fusion.4), calls=%async_computation | async-start | bytes 3538944 | tf_op jit(solution)/shard_map/all_to_all | solution.py:30
  114.6 3.9 %multiply_reduce_fusion.1 = (f32[6,256]{1,0:T(8,128)S(1)}, f32[6,256,1152]{2,1,0:T(8,128)}) fusion(bf16[6,256,128]{2,1,0:T(8,128)(2,1)S(1)} %bitcast.165, bf16[6,1152,128]{2,1,0:T(8,128)(2,1)S(1)} %bitcast.152), kind=kOutput, calls=%fused_computation.38 | convolution fusion | flops 456522240 | bytes 9246720 | tf_op jit(solution)/shard_map/hqd,hkd->hqk/dot_general | solution.py:95
  118.5 17.3 %pmax.7 = f32[6,256]{1,0:T(8,128)} all-reduce(f32[6,256]{1,0:T(8,128)S(1)} %get-tuple-element.100), channel_id=1, replica_groups=mesh['uly'=4,'blk'=8] {'blk'}, use_global_device_ids=true, to_apply=%region_7.9 | all-reduce | flops 1536 | bytes 12288 | tf_op jit(solution)/shard_map/pmax | solution.py:103
  136.5 5.5 %fusion.24 = f32[6,256,128]{2,1,0:T(8,128)} fusion(bf16[6,1152,128]{2,1,0:T(8,128)(2,1)S(1)} %bitcast.155, f32[6,256,1152]{2,1,0:T(8,128)} %get-tuple-element.101, f32[6,256]{1,0:T(8,128)S(1)} %max.12), kind=kOutput, calls=%fused_computation.41 | convolution fusion | flops 458293248 | bytes 9639936 | tf_op jit(solution)/shard_map/hqk,hkd->hqd/dot_general | solution.py:106
  142.0 5.0 %fusion.22 = f32[6,256]{1,0:T(8,128)} fusion(f32[6,256,1152]{2,1,0:T(8,128)} %get-tuple-element.101, f32[6,256]{1,0:T(8,128)S(1)} %max.12), kind=kLoop, calls=%fused_computation.39 | loop fusion | flops 5306880 | bytes 7090176 | tf_op jit(solution)/shard_map/reduce_sum | solution.py:112
  149.9 14.8 %psum.15 = f32[6,256]{1,0:T(8,128)} all-reduce(f32[6,256]{1,0:T(8,128)} %fusion.22), channel_id=1, replica_groups=mesh['uly'=4,'blk'=8] {'blk'}, use_global_device_ids=true, to_apply=%region_11.13 | all-reduce | flops 1536 | bytes 12288 | tf_op jit(solution)/shard_map/psum | solution.py:112
  167.7 30.2 %all-reduce.2.cloned.1.call-done = f32[6,256,128]{2,1,0:T(8,128)} async-done(((f32[6,256,128]{2,1,0:T(8,128)}), f32[6,256,128]{2,1,0:T(8,128)}) %all-reduce.2.cloned.1.call-update) | async-done | bytes 786448 | tf_op jit(solution)/shard_map/psum | solution.py:112
  201.3 4.3 %all-to-all-start.7 = ((bf16[256,6,128]{2,1,0:T(8,128)(2,1)}), bf16[256,6,128]{2,1,0:T(8,128)(2,1)}, u32[]{:S(2)}, u32[]{:S(2)}) async-start(bf16[256,6,128]{2,1,0:T(8,128)(2,1)} %copy.55), calls=%async_computation.7 | async-start | bytes 1048576 | tf_op jit(solution)/shard_map/all_to_all | solution.py:124
  205.6 8.0 %pad_maximum_fusion = bf16[2,6,3456,128]{3,2,1,0:T(8,128)(2,1)} fusion(bf16[2,6,1152,128]{3,2,1,0:T(8,128)(2,1)} %collective-permute-done.1, bf16[1,6,1152,128]{3,2,1,0:T(8,128)(2,1)S(1)} %bitcast.156, bf16[1,6,1152,128]{3,2,1,0:T(8,128)(2,1)S(1)} %bitcast.153, bf16[2,6,1152,128]{3,2,1,0:T(8,128)(2,1)} %collective-permute-done), kind=kLoop, calls=%fused_computation.36 | loop fusion | flops 42467328 | bytes 21233664 | tf_op jit(solution)/shard_map/concatenate | solution.py:51
  213.6 8.8 %fusion.37 = (bf16[1,6,3456,128]{3,2,1,0:T(8,128)(2,1)}, bf16[1,6,3456,128]{3,2,1,0:T(8,128)(2,1)}) fusion(bf16[2,6,3456,128]{3,2,1,0:T(8,128)(2,1)} %pad_maximum_fusion), kind=kLoop, calls=%fused_computation.67 | loop fusion | bytes 21233664 | tf_op jit(solution)/shard_map/slice | solution.py:92
  222.4 106.2 %while.11 = (s32[]{:T(128)}, bf16[6,1152,128]{2,1,0:T(8,128)(2,1)}, bf16[6,1152,128]{2,1,0:T(8,128)(2,1)}, bf16[6,9,384,128]{3,2,1,0:T(8,128)(2,1)}, s32[3,6]{1,...) while((s32[]{:T(128)}, bf16[6,1152,128]{2,1,0:T(8,128)(2,1)}, ...), condition=%wide.region_5.7_spmd.clone, body=%wide.region_0.6_spmd.clone.sunk | while | flops 1535458432 | bytes 60074196 | solution.py:91
  328.6 7.7 %copy.75 = bf16[6,1152,128]{2,0,1:T(8,128)(2,1)} copy(bf16[6,1152,128]{2,1,0:T(8,128)(2,1)} %get-tuple-element.50) | data formatting | bytes 3538944 | tf_op jit(solution)/shard_map/while | solution.py:91
  336.3 4.5 %all-to-all-start.5 = ((bf16[1152,6,128]{2,1,0:T(8,128)(2,1)}), bf16[1152,6,128]{2,1,0:T(8,128)(2,1)}, u32[]{:S(2)}, u32[]{:S(2)}) async-start(bf16[1152,6,128]{2,1,0:T(8,128)(2,1)} %bitcast.159), calls=%async_computation.5 | async-start | bytes 4718592 | tf_op jit(solution)/shard_map/all_to_all | solution.py:123
  343.1 24.0 %all-to-all-done.5 = bf16[1152,6,128]{2,1,0:T(8,128)(2,1)} async-done(((bf16[1152,6,128]{2,1,0:T(8,128)(2,1)}), bf16[1152,6,128]{2,1,0:T(8,128)(2,1)}, u32[]{:S(2)}, u32[]{:S(2)}) %all-to-all-start.5) | async-done | bytes 1769504 | tf_op jit(solution)/shard_map/all_to_all | solution.py:123
  370.6 4.7 %reshape.69 = bf16[288,3072]{1,0:T(8,128)(2,1)} reshape(bf16[288,4,6,128]{3,2,1,0:T(8,128)(2,1)} %bitcast.160) | data formatting | bytes 3538944 | tf_op jit(solution)/shard_map/reshape | solution.py:126
  (160 shorter events, 150.6 us)
Async XLA Ops:
  7.2 1.5 copy-start
  10.2 5.3 %copy-start.3 = (bf16[288,3072]{1,0:T(8,128)(2,1)S(1)}, bf16[288,3072]{1,0:T(8,128)(2,1)}, u32[]{:S(2)}) copy-start(bf16[288,3072]{1,0:T(8,128)(2,1)} %param.14) | copy-start | bytes 5308420
  10.2 26.7 %all-to-all-start.1 = ((bf16[288,24,128]{2,0,1:T(8,128)(2,1)}), bf16[288,24,128]{2,0,1:T(8,128)(2,1)S(1)}, u32[]{:S(2)}, u32[]{:S(2)}) async-start(bf16[288,24,128]{2,0,1:T(8,128)(2,1)} %copy_bitcast_fusion.3), calls=%async_computation.1 | async-start | bytes 3538944 | tf_op jit(solution)/shard_map/all_to_all | solution.py:31
  36.8 25.3 %all-to-all-start.2 = ((bf16[288,24,128]{2,0,1:T(8,128)(2,1)}), bf16[288,24,128]{2,0,1:T(8,128)(2,1)}, u32[]{:S(2)}, u32[]{:S(2)}) async-start(bf16[288,24,128]{2,0,1:T(8,128)(2,1)} %copy_bitcast_fusion.2), calls=%async_computation.2 | async-start | bytes 3538944 | tf_op jit(solution)/shard_map/all_to_all | solution.py:32
  63.7 6.6 %copy-start.4 = (bf16[64,3072]{1,0:T(8,128)(2,1)S(1)}, bf16[64,3072]{1,0:T(8,128)(2,1)}, u32[]{:S(2)}) copy-start(bf16[64,3072]{1,0:T(8,128)(2,1)} %param.15) | copy-start | bytes 1179652
  63.7 11.5 %copy-start.5 = (s32[3,6]{1,0:T(4,128)S(1)}, s32[3,6]{1,0:T(4,128)}, u32[]{:S(2)}) copy-start(s32[3,6]{1,0:T(4,128)} %param.18) | copy-start | bytes 220
  65.9 139.7 %collective-permute-start = (bf16[2,6,1152,128]{3,2,1,0:T(8,128)(2,1)}, bf16[2,6,1152,128]{3,2,1,0:T(8,128)(2,1)}, u32[]{:S(2)}, u32[]{:S(2)}) collective-permute-start(bf16[2,6,1152,128]{3,2,1,0:T(8,128)(2,1)} %pad_maximum_fusion.1), channel_id=1, source_target_pairs={{0,1},{1,2},{2,3},{3,4},{4,5},{5,6},{6,7},{8,9},{9,10},{10,11},{11... | collective-permute-start | bytes 10616840 | tf_op jit(solution)/shard_map/ppermute | solution.py:16
  69.0 136.6 %collective-permute-start.1 = (bf16[2,6,1152,128]{3,2,1,0:T(8,128)(2,1)}, bf16[2,6,1152,128]{3,2,1,0:T(8,128)(2,1)}, u32[]{:S(2)}, u32[]{:S(2)}) collective-permute-start(bf16[2,6,1152,128]{3,2,1,0:T(8,128)(2,1)} %pad_maximum_fusion.1), channel_id=1, source_target_pairs={{1,0},{2,1},{3,2},{4,3},{5,4},{6,5},{7,6},{9,8},{10,9},{11,10},{12... | collective-permute-start | bytes 10616840 | tf_op jit(solution)/shard_map/ppermute | solution.py:16
  71.2 11.9 %all-to-all-start.6 = ((bf16[64,24,128]{2,0,1:T(8,128)(2,1)}), bf16[64,24,128]{2,0,1:T(8,128)(2,1)}, u32[]{:S(2)}, u32[]{:S(2)}) async-start(bf16[64,24,128]{2,0,1:T(8,128)(2,1)} %copy_bitcast_fusion.6), calls=%async_computation.6 | async-start | bytes 786432 | tf_op jit(solution)/shard_map/all_to_all | solution.py:33
  83.0 11.4 %all-to-all-start.3 = ((bf16[64,24,128]{2,0,1:T(8,128)(2,1)}), bf16[64,24,128]{2,0,1:T(8,128)(2,1)}, u32[]{:S(2)}, u32[]{:S(2)}) async-start(bf16[64,24,128]{2,0,1:T(8,128)(2,1)} %copy_bitcast_fusion.8), calls=%async_computation.3 | async-start | bytes 786432 | tf_op jit(solution)/shard_map/all_to_all | solution.py:34
  94.4 10.7 %all-to-all-start.4 = ((bf16[64,24,128]{2,0,1:T(8,128)(2,1)}), bf16[64,24,128]{2,0,1:T(8,128)(2,1)}, u32[]{:S(2)}, u32[]{:S(2)}) async-start(bf16[64,24,128]{2,0,1:T(8,128)(2,1)} %copy_bitcast_fusion.7), calls=%async_computation.4 | async-start | bytes 786432 | tf_op jit(solution)/shard_map/all_to_all | solution.py:35
  105.1 41.9 %all-to-all-start = ((bf16[288,24,128]{2,0,1:T(8,128)(2,1)}), bf16[288,24,128]{2,0,1:T(8,128)(2,1)}, u32[]{:S(2)}, u32[]{:S(2)}) async-start(bf16[288,24,128]{2,0,1:T(8,128)(2,1)} %copy_bitcast_fusion.4), calls=%async_computation | async-start | bytes 3538944 | tf_op jit(solution)/shard_map/all_to_all | solution.py:30
  109.5 88.4 %all-reduce.2.cloned.1.call-start = ((), (), s32[]{:S(2)}) async-start(), calls=%async_computation.8 | async-start | bytes 1572864 | tf_op jit(solution)/shard_map/psum | solution.py:112
  109.5 5.1 %copy-start.2 = (bf16[4,64,6,128]{3,1,0,2:T(8,128)(2,1)S(1)}, bf16[4,64,6,128]{3,1,0,2:T(8,128)(2,1)}, u32[]{:S(2)}) copy-start(bf16[4,64,6,128]{3,1,0,2:T(8,128)(2,1)} %copy.53) | copy-start | bytes 1179652
  201.3 135.1 %all-to-all-start.7 = ((bf16[256,6,128]{2,1,0:T(8,128)(2,1)}), bf16[256,6,128]{2,1,0:T(8,128)(2,1)}, u32[]{:S(2)}, u32[]{:S(2)}) async-start(bf16[256,6,128]{2,1,0:T(8,128)(2,1)} %copy.55), calls=%async_computation.7 | async-start | bytes 1048576 | tf_op jit(solution)/shard_map/all_to_all | solution.py:124
  336.3 30.8 %all-to-all-start.5 = ((bf16[1152,6,128]{2,1,0:T(8,128)(2,1)}), bf16[1152,6,128]{2,1,0:T(8,128)(2,1)}, u32[]{:S(2)}, u32[]{:S(2)}) async-start(bf16[1152,6,128]{2,1,0:T(8,128)(2,1)} %bitcast.159), calls=%async_computation.5 | async-start | bytes 4718592 | tf_op jit(solution)/shard_map/all_to_all | solution.py:123
  370.6 4.7 %copy-start.1 = (bf16[288,3072]{1,0:T(8,128)(2,1)S(1)}, bf16[288,3072]{1,0:T(8,128)(2,1)}, u32[]{:S(2)}) copy-start(bf16[288,3072]{1,0:T(8,128)(2,1)} %param.13) | copy-start | bytes 5308420
Sparse Core Ops, SparseCore 0:
  142.1 55.6 all-reduce.1
where the time goes:
time: 385 us; the launch traced here: 382 us
  waiting for transfers between devices  105 us (27%)
  local copies, waits for them, and re-layouts  88.4 us (23%)
  matrix products  54.9 us (14%)
  other arithmetic  46.4 us (12%)
  starting transfers between devices  39.6 us (10%)
  blocking collectives  32.1 us (8%)
  between operations  14.9 us (4%)
    psum x1, waiting for transfers between devices, local(): lax.psum((jnp.sum(vid_weights, axis=2), vid_numer), 'blk')  30.2 us
    all_to_all x1, waiting for transfers between devices, local(): lax.all_to_all(head_major(video_heads), 'uly', split_axis=0, concat_axis=...  24 us
    all_to_all x1, waiting for transfers between devices, local(): lax.all_to_all(split_heads(video_v), 'uly', split_axis=1, concat_axis=0,...  20.7 us
    all_to_all x1, waiting for transfers between devices, local(): lax.all_to_all(split_heads(video_k), 'uly', split_axis=1, concat_axis=0,...  19.8 us
    pmax x1, blocking collectives, local(): video_top = lax.pmax(jnp.max(vid_scores, axis=2), 'blk')  17.3 us
    dot_general x6, matrix products, video_attention(): jnp.einsum('tqk,tkd->tqd', win_weights.astype(jnp.bfloat16), values_win,...  15.3 us
    psum x1, blocking collectives, local(): lax.psum((jnp.sum(vid_weights, axis=2), vid_numer), 'blk')  14.8 us
    gather x6, local copies, waits for them, and re-layouts, video_attention(): jnp.take(values_all, local_tiles, axis=0)  12.6 us
  transfers between devices with their start and end apart: 11, of which 6 were waited for; matrix products, arithmetic and copies ran while one was open for 46% of the time, Pallas kernels for 0%

commit v1 on v0

v1 whole, which is shorter than its diff:
```python
import functools
import math

import jax
import jax.numpy as jnp
from jax import lax
from jax.experimental import pallas as pl
from jax.experimental.pallas import tpu as pltpu
from jax.sharding import PartitionSpec as P

D = 128
TILE = 384
PIECE = 32
MESH = pl.DeviceIdType.MESH
NEG = -jnp.inf
SCALE = math.log2(math.e) / math.sqrt(D)


def dot_t(a, b):
    return lax.dot_general(a, b, (((1,), (1,)), ((), ())), preferred_element_type=jnp.float32)


def dot(a, b):
    return jnp.dot(a, b, preferred_element_type=jnp.float32)


def kernel(
    n_u, n_b, heads, rows, trows,
    vq, vk, vv, tq, tk, tv, win, tlen,
    vout, tout,
    qb, kb, vb, kp, vp, kn, vn, ob, tqb, tkb, tvb, po, pml, ro, rml, fin,
    xs, xr, ts, tr, hs, hr, os_, or_, ps, pr, fs, fr,
):
    u = lax.axis_index("uly")
    b = lax.axis_index("blk")
    width = heads * D
    tiles = n_u * rows // TILE
    text = n_u * trows
    pieces = text // PIECE
    per_u = trows // PIECE
    has_prev = b > 0
    has_next = b < n_b - 1

    def to_uly(r):
        return lax.rem(u + r, n_u)

    def from_uly(r):
        return lax.rem(u + n_u - r, n_u)

    def remote(src, dst, s, r, uly, blk):
        return pltpu.make_async_remote_copy(
            src_ref=src, dst_ref=dst, send_sem=s, recv_sem=r,
            device_id=(blk, uly) if AXES[0] == "blk" else (uly, blk), device_id_type=MESH,
        )

    video = ((vk, kb), (vv, vb), (vq, qb))
    texts = ((tq, tqb), (tk, tkb), (tv, tvb))

    def x_copy(i, h, r, dest, src):
        a, buf = video[i]
        source = a.at[:, pl.ds(pl.multiple_of((dest * heads + h) * D, D), D)]
        target = buf.at[h, pl.ds(pl.multiple_of(src * rows, 16), rows), :]
        return source, target, xs.at[i, h, r], xr.at[i, h, r]

    def x_start(i, h):
        for r in range(1, n_u):
            remote(*x_copy(i, h, r, to_uly(r), u), to_uly(r), b).start()
        s, t, _, sem = x_copy(i, h, 0, u, u)
        pltpu.make_async_copy(s, t, sem).start()

    def x_wait(i, h):
        s, t, _, sem = x_copy(i, h, 0, u, u)
        pltpu.make_async_copy(s, t, sem).wait()
        for r in range(1, n_u):
            remote(*x_copy(i, h, r, to_uly(r), from_uly(r)), to_uly(r), b).wait_recv()

    def t_copy(i, r, dest, src):
        a, buf = texts[i]
        source = a.at[:, pl.ds(pl.multiple_of(dest * width, D), width)]
        target = buf.at[pl.ds(pl.multiple_of(src * trows, 16), trows), :]
        return source, target, ts.at[i, r], tr.at[i, r]

    def halo(h, i):
        src = (kb, vb)[i % 2]
        dst = (kp, vp, kn, vn)[i]
        blk = b + 1 if i < 2 else b - 1
        return remote(src.at[h], dst.at[h], hs.at[h, i], hr.at[h, i], u, blk)

    def halo_each(h, first, second, what):
        for cond, ids in ((first, (0, 1)), (second, (2, 3))):
            @pl.when(cond)
            def _():
                for i in ids:
                    what(halo(h, i))

    def o_copy(h, r, dest, src):
        source = ob.at[h, pl.ds(pl.multiple_of(dest * rows, 16), rows), :]
        target = vout.at[:, pl.ds(pl.multiple_of((src * heads + h) * D, D), D)]
        return source, target, os_.at[h, r], or_.at[h, r]

    for i in range(3):
        for r in range(1, n_u):
            remote(*t_copy(i, r, to_uly(r), u), to_uly(r), b).start()
        s, t, _, sem = t_copy(i, 0, u, u)
        pltpu.make_async_copy(s, t, sem).start()

    def start_head(h, c):
        for i in range(3):
            x_start(i, h)
        return c

    lax.fori_loop(0, heads, start_head, 0)

    for i in range(3):
        s, t, _, sem = t_copy(i, 0, u, u)
        pltpu.make_async_copy(s, t, sem).wait()
        for r in range(1, n_u):
            remote(*t_copy(i, r, to_uly(r), from_uly(r)), to_uly(r), b).wait_recv()

    live = tlen[0]
    lane = lax.broadcasted_iota(jnp.int32, (1, text), 1)
    video_bias = jnp.where(lane < live, 0.0, NEG)
    text_bias = jnp.where(lane < jnp.where(b == 0, live, 0), 0.0, NEG)
    lane8 = lax.broadcasted_iota(jnp.int32, (1, D), 1) // 8

    def arrive(h):
        x_wait(0, h)
        x_wait(1, h)
        halo_each(h, has_next, has_prev, lambda c: c.start())
        cols = pl.ds(pl.multiple_of(h * D, D), D)
        q = tqb[:, cols]
        s1 = dot_t(q, kb[h])
        s2 = dot_t(q, tkb[:, cols]) + text_bias
        m = jnp.maximum(jnp.max(s1, axis=1, keepdims=True), jnp.max(s2, axis=1, keepdims=True))
        p1 = jnp.exp2((s1 - m) * SCALE)
        p2 = jnp.exp2((s2 - m) * SCALE)
        total = jnp.sum(p1, axis=1, keepdims=True) + jnp.sum(p2, axis=1, keepdims=True)
        o = dot(p1.astype(jnp.bfloat16), vb[h]) + dot(p2.astype(jnp.bfloat16), tvb[:, cols])
        po[h] = o.astype(jnp.bfloat16)
        pml[...] = jnp.where(lane8 == 2 * h, m, jnp.where(lane8 == 2 * h + 1, total, pml[...]))

    def attend(h):
        x_wait(2, h)
        halo_each(h, has_prev, has_next, lambda c: c.wait_recv())
        cols = pl.ds(pl.multiple_of(h * D, D), D)

        def tile(t, c):
            last = win[t, 0]
            for w in range(1, win.shape[1]):
                last = jnp.maximum(last, win[t, w])
            after = last >= (b + 1) * tiles
            at = pl.ds(pl.multiple_of(t * TILE, 16), TILE)
            q = qb[h, at, :]
            s1 = dot_t(q, kb[h])
            s2 = dot_t(q, jnp.where(after, kn[h], kp[h]))
            s3 = dot_t(q, tkb[:, cols]) + video_bias
            m = jnp.maximum(jnp.max(s1, axis=1, keepdims=True), jnp.max(s2, axis=1, keepdims=True))
            m = jnp.maximum(m, jnp.max(s3, axis=1, keepdims=True))
            p1 = jnp.exp2((s1 - m) * SCALE)
            p2 = jnp.exp2((s2 - m) * SCALE)
            p3 = jnp.exp2((s3 - m) * SCALE)
            total = (
                jnp.sum(p1, axis=1, keepdims=True)
                + jnp.sum(p2, axis=1, keepdims=True)
                + jnp.sum(p3, axis=1, keepdims=True)
            )
            o = dot(p1.astype(jnp.bfloat16), vb[h])
            o = o + dot(p2.astype(jnp.bfloat16), jnp.where(after, vn[h], vp[h]))
            o = o + dot(p3.astype(jnp.bfloat16), tvb[:, cols])
            ob[h, at, :] = (o / total).astype(jnp.bfloat16)
            return c

        lax.fori_loop(0, tiles, tile, 0)
        for r in range(1, n_u):
            remote(*o_copy(h, r, to_uly(r), u), to_uly(r), b).start()
        s, t, _, sem = o_copy(h, 0, u, u)
        pltpu.make_async_copy(s, t, sem).start()

    def p_copies(r, dest, src):
        at = pl.ds(pl.multiple_of(dest * PIECE, PIECE), PIECE)
        return (
            (po.at[:, at, :], ro.at[src], ps.at[0, r], pr.at[0, r]),
            (pml.at[at, :], rml.at[src], ps.at[1, r], pr.at[1, r]),
        )

    def to_blk(r):
        return lax.rem(b + r, n_b)

    def from_blk(r):
        return lax.rem(b + n_b - r, n_b)

    def p_start():
        for r in range(1, n_b):
            @pl.when(to_blk(r) < pieces)
            def _():
                for c in p_copies(r, to_blk(r), b):
                    remote(*c, u, to_blk(r)).start()
        @pl.when(b < pieces)
        def _():
            for s, t, _, sem in p_copies(0, b, b):
                pltpu.make_async_copy(s, t, sem).start()

    owner = b // per_u
    my_rows = pl.ds(pl.multiple_of(lax.rem(b, per_u) * PIECE, PIECE), PIECE)

    def f_out(r):
        slot = u * per_u + lax.rem(b, per_u)
        target = tout.at[my_rows, pl.ds(pl.multiple_of(u * width, D), width)]
        return (fin, target, fs.at[r], fr.at[slot])

    def f_each(what_remote, what_local):
        for r in range(n_b):
            if r == 0:
                @pl.when(owner == u)
                def _():
                    if what_local is not None:
                        s, t, _, sem = f_out(0)
                        what_local(pltpu.make_async_copy(s, t, sem))

                @pl.when(owner != u)
                def _():
                    what_remote(remote(*f_out(0), owner, b))
            else:
                what_remote(remote(*f_out(r), owner, to_blk(r)))

    def merge():
        for r in range(1, n_b):
            for c in p_copies(r, b, from_blk(r)):
                remote(*c, u, to_blk(r)).wait_recv()
        for s, t, _, sem in p_copies(0, b, b):
            pltpu.make_async_copy(s, t, sem).wait()
        ml = rml[...]
        lanes = lane8[None]
        for h in range(heads):
            m = jnp.max(jnp.where(lanes == 2 * h, ml, NEG), axis=2, keepdims=True)
            total = jnp.max(jnp.where(lanes == 2 * h + 1, ml, 0.0), axis=2, keepdims=True)
            w = jnp.exp2((m - jnp.max(m, axis=0, keepdims=True)) * SCALE)
            o = jnp.sum(ro[:, h].astype(jnp.float32) * w, axis=0)
            fin[:, h * D:(h + 1) * D] = (o / jnp.sum(total * w, axis=0)).astype(jnp.bfloat16)
        f_each(lambda c: c.start(), lambda c: c.start())

    pml[...] = jnp.zeros_like(pml)
    arrive(0)

    def step(h, c):
        @pl.when(h < heads - 1)
        def _():
            arrive(h + 1)

        @pl.when(h == heads - 2)
        def _():
            p_start()

        @pl.when(h == heads - 1)
        def _():
            pl.when(b < pieces)(merge)

        attend(h)
        return c

    lax.fori_loop(0, heads, step, 0)

    def finish(h, c):
        s, t, _, sem = o_copy(h, 0, u, u)
        pltpu.make_async_copy(s, t, sem).wait()
        for r in range(1, n_u):
            remote(*o_copy(h, r, to_uly(r), from_uly(r)), to_uly(r), b).wait_recv()
            remote(*o_copy(h, r, to_uly(r), u), to_uly(r), b).wait_send()
            for i in range(3):
                remote(*x_copy(i, h, r, to_uly(r), u), to_uly(r), b).wait_send()
        halo_each(h, has_next, has_prev, lambda c: c.wait_send())
        return c

    lax.fori_loop(0, heads, finish, 0)
    for i in range(3):
        for r in range(1, n_u):
            remote(*t_copy(i, r, to_uly(r), u), to_uly(r), b).wait_send()
    for r in range(1, n_b):
        @pl.when(to_blk(r) < pieces)
        def _():
            for c in p_copies(r, to_blk(r), b):
                remote(*c, u, to_blk(r)).wait_send()

    @pl.when(b < pieces)
    def _():
        f_each(lambda c: c.wait_send(), None)

    for su in range(n_u):
        for k in range(per_u):
            slot = su * per_u + k
            target = tout.at[k * PIECE:(k + 1) * PIECE, su * width:(su + 1) * width]
            pltpu.make_async_copy(fin, target, fr.at[slot]).wait()


AXES = ["uly", "blk"]


def local(n_u, n_b, *args):
    vq, _, _, tq = args[:4]
    rows, cols = vq.shape
    trows = tq.shape[0]
    heads = cols // D // n_u
    seq, text = rows * n_u, trows * n_u
    bf = jnp.bfloat16
    dma = pltpu.SemaphoreType.DMA
    slab = pltpu.VMEM((heads, seq, D), bf)
    tslab = pltpu.VMEM((text, heads * D), bf)
    hbm = pl.BlockSpec(memory_space=pl.ANY)
    smem = pl.BlockSpec(memory_space=pltpu.SMEM)
    slots = n_u * (trows // PIECE)
    return pl.pallas_call(
        functools.partial(kernel, n_u, n_b, heads, rows, trows),
        out_shape=(
            jax.ShapeDtypeStruct((rows, cols), bf),
            jax.ShapeDtypeStruct((trows, cols), bf),
        ),
        in_specs=[hbm] * 6 + [smem] * 2,
        out_specs=(hbm, hbm),
        scratch_shapes=[slab] * 8 + [tslab] * 3 + [
            pltpu.VMEM((heads, text, D), bf),
            pltpu.VMEM((text, D), jnp.float32),
            pltpu.VMEM((n_b, heads, PIECE, D), bf),
            pltpu.VMEM((n_b, PIECE, D), jnp.float32),
            pltpu.VMEM((PIECE, heads * D), bf),
            dma((3, heads, n_u)), dma((3, heads, n_u)),
            dma((3, n_u)), dma((3, n_u)),
            dma((heads, 4)), dma((heads, 4)),
            dma((heads, n_u)), dma((heads, n_u)),
            dma((2, n_b)), dma((2, n_b)),
            dma((n_b,)), dma((slots,)),
        ],
        compiler_params=pltpu.CompilerParams(
            has_side_effects=True, vmem_limit_bytes=56 * 2**20
        ),
    )(*args)


def solution(mesh):
    AXES[:] = mesh.axis_names
    in_specs = (
        P(("blk", "uly"), None),
        P(("blk", "uly"), None),
        P(("blk", "uly"), None),
        P("uly", None),
        P("uly", None),
        P("uly", None),
        P("blk", None),
        P(),
    )
    out_specs = (P(("blk", "uly"), None), P("uly", None))
    body = functools.partial(local, mesh.shape["uly"], mesh.shape["blk"])
    return jax.shard_map(body, mesh=mesh, in_specs=in_specs, out_specs=out_specs, check_vma=False)
```

time: 385 us -> 118 us (0.31)
  Pallas kernels: 0 us -> 112 us
  waiting for transfers between devices: 105 us -> 0 us
  local copies, waits for them, and re-layouts: 88.4 us -> 3.6 us
  matrix products: 54.9 us -> 0 us
  other arithmetic: 46.4 us -> 0 us
  starting transfers between devices: 39.6 us -> 0 us
  blocking collectives: 32.1 us -> 0 us
  between operations: 14.9 us -> 1.3 us
    pallas_call x0 -> x1, Pallas kernels: none -> 112 us  [local(): pl.pallas_call(functools.partial(kernel, n_u, n_b, heads, rows, trows), o...]
    all_to_all x8 -> x0, waiting for transfers between devices: 75.2 us -> none  [the longest x1 24 us: local(): lax.all_to_all(head_major(video_heads), 'uly', split_axis=0, concat_axis=...]
    dot_general x28 -> x0, matrix products: 54.9 us -> none  [the longest x6 15.3 us: video_attention(): jnp.einsum('tqk,tkd->tqd', win_weights.astype(jnp.bfloat16), values_win,...]
    all_to_all x8 -> x0, starting transfers between devices: 35.2 us -> none  [the longest x1 5.29 us: local(): lax.all_to_all(split_heads(video_k), 'uly', split_axis=1, concat_axis=0,...]
    psum x1 -> x0, waiting for transfers between devices: 30.2 us -> none  [local(): lax.psum((jnp.sum(vid_weights, axis=2), vid_numer), 'blk')]
    reduce_sum x14 -> x0, other arithmetic: 19 us -> none  [the longest x12 12.4 us: video_attention(): weight_sum = jnp.sum(win_weights, axis=2) + jnp.sum(txt_weights, axis=2)]
    gather x12 -> x0, local copies, waits for them, and re-layouts: 18 us -> none  [the longest x6 12.6 us: video_attention(): jnp.take(values_all, local_tiles, axis=0)]
    pmax x1 -> x0, blocking collectives: 17.3 us -> none  [local(): video_top = lax.pmax(jnp.max(vid_scores, axis=2), 'blk')]
  transfers between devices with their start and end apart: 11 -> 0, of which waited for: 6 -> 0; matrix products, arithmetic and copies ran while one was open for 46% -> 0% of each run, Pallas kernels for 0% -> 0%
where the time goes in v1:
time: 118 us; the launch traced here: 117 us
  Pallas kernels  112 us (95%)
  local copies, waits for them, and re-layouts  3.6 us (3%)
  between operations  1.3 us (1%)
    pallas_call x1, Pallas kernels, local(): pl.pallas_call(functools.partial(kernel, n_u, n_b, heads, rows, trows), o...  112 us
    unnamed x4, local copies, waits for them, and re-layouts  3.6 us

profile of v1, /device:TPU:0, one launch (start us, length us, event | category | flops | bytes accessed | tf_op | source)
XLA Modules:
  0.0 116.6 jit_solution(15965360568548289462)
XLA Ops:
  1.3 111.7 %shard_map.95 = (bf16[288,3072]{1,0:T(8,128)(2,1)}, bf16[64,3072]{1,0:T(8,128)(2,1)}) custom-call(bf16[288,3072]{1,0:T(8,128)(2,1)} %vq.1, bf16[288,3072]{1,0:T(8,128)(2,1)} %vk.1, bf16[288,3072]{1,0:T(8,128)(2,1)} %vv.1, bf16[64,3072]{1,0:T(8,128)(2,1)} %tq.1, bf16[64,3072]{1,0:T(8,128)(2,1)} %tk.1, bf16[64,3072]{1,0:T(8,128)(2,1)} %tv.1, s32[3,6]{1,0:T(4,128)} %win.1, ...), custom_call_target="tpu_custom_call" | custom-call | tf_op jit(solution)/shard_map/pallas_call | solution.py:311
  113.0 0.0 copy-start
  113.0 2.8 %copy.13 = bf16[288,3072]{1,0:T(8,128)(2,1)} copy(bf16[288,3072]{1,0:T(8,128)(2,1)} %get-tuple-element.4) | data formatting | bytes 3538944
  115.8 0.0 copy-done
  115.8 0.7 copy.14
Async XLA Ops:
  113.0 2.9 %copy-start = (bf16[64,3072]{1,0:T(8,128)(2,1)S(1)}, bf16[64,3072]{1,0:T(8,128)(2,1)}, u32[]{:S(2)}) copy-start(bf16[64,3072]{1,0:T(8,128)(2,1)} %get-tuple-element.5) | copy-start | bytes 1179652
